TPU v7x, 32 devices: a whole 2x2x4 slice. The times are simulated.
32 devices in a mesh: section: 2 (over core), img: 4 (over z), row: 4 (over y, x).
Axes of the slice: x: 2, y: 2, z: 4, core: 2. Of those that a mesh axis runs over, the one named last changes fastest.
Arguments:
- input_maps: bfloat16 [8, 4, 32, 32, 192], P(None, 'img', 'row'), may hold values from -6 to 6
- valid_rows: int32 [8, 4], P(None, 'img'), may hold values from 17 to 32, as said below
- valid_cols: int32 [8, 4], P(None, 'img'), may hold values from 17 to 32, as said below
- first_reduce: bfloat16 [192, 512], replicated, may hold values from -0.4375 to 0.4375
- first_reduce_gain: bfloat16 [512], replicated, may hold values from 0.5 to 1.5
- first_reduce_shift: bfloat16 [512], replicated, may hold values from -3 to 3
- first_groups: bfloat16 [9, 8, 64, 64], replicated, may hold values from -0.25 to 0.25
- first_groups_gain: bfloat16 [512], replicated, may hold values from 0.5 to 1.5
- first_groups_shift: bfloat16 [512], replicated, may hold values from -3 to 3
- first_squeeze: bfloat16 [512, 48], replicated, may hold values from -0.75 to 0.75
- first_squeeze_bias: bfloat16 [48], replicated, may hold values from -3 to 3
- first_excite: bfloat16 [48, 512], replicated, may hold values from -1.75 to 1.75
- first_excite_bias: bfloat16 [512], replicated, may hold values from -4 to 4
- first_expand: bfloat16 [512, 512], replicated, may hold values from -0.25 to 0.25
- first_expand_gain: bfloat16 [512], replicated, may hold values from 0.5 to 1.5
- first_expand_shift: bfloat16 [512], replicated, may hold values from -3 to 3
- first_shortcut: bfloat16 [192, 512], replicated, may hold values from -0.4375 to 0.4375
- first_shortcut_gain: bfloat16 [512], replicated, may hold values from 0.5 to 1.5
- first_shortcut_shift: bfloat16 [512], replicated, may hold values from -3 to 3
- second_reduce: bfloat16 [512, 512], replicated, may hold values from -0.25 to 0.25
- second_reduce_gain: bfloat16 [512], replicated, may hold values from 0.5 to 1.5
- second_reduce_shift: bfloat16 [512], replicated, may hold values from -3 to 3
- second_groups: bfloat16 [9, 8, 64, 64], replicated, may hold values from -0.25 to 0.25
- second_groups_gain: bfloat16 [512], replicated, may hold values from 0.5 to 1.5
- second_groups_shift: bfloat16 [512], replicated, may hold values from -3 to 3
- second_squeeze: bfloat16 [512, 128], replicated, may hold values from -0.75 to 0.75
- second_squeeze_bias: bfloat16 [128], replicated, may hold values from -3 to 3
- second_excite: bfloat16 [128, 512], replicated, may hold values from -1 to 1
- second_excite_bias: bfloat16 [512], replicated, may hold values from -4 to 4
- second_expand: bfloat16 [512, 512], replicated, may hold values from -0.25 to 0.25
- second_expand_gain: bfloat16 [512], replicated, may hold values from 0.5 to 1.5
- second_expand_shift: bfloat16 [512], replicated, may hold values from -3 to 3
- output_grad: bfloat16 [8, 4, 16, 16, 512], P(None, 'img', 'row'), may hold values from -6 to 6
Outputs:
- activations: bfloat16 [2, 8, 4, 16, 16, 512], P('section', None, 'img', 'row')
- input_gradient: bfloat16 [8, 4, 32, 32, 192], P(None, 'img', 'row', None, 'section')
- grad_first_reduce: float32 [192, 512], replicated
- grad_first_reduce_gain: float32 [512], replicated
- grad_first_reduce_shift: float32 [512], replicated
- grad_first_groups: float32 [9, 8, 64, 64], replicated
- grad_first_groups_gain: float32 [512], replicated
- grad_first_groups_shift: float32 [512], replicated
- grad_first_squeeze: float32 [512, 48], replicated
- grad_first_squeeze_bias: float32 [48], replicated
- grad_first_excite: float32 [48, 512], replicated
- grad_first_excite_bias: float32 [512], replicated
- grad_first_expand: float32 [512, 512], replicated
- grad_first_expand_gain: float32 [512], replicated
- grad_first_expand_shift: float32 [512], replicated
- grad_first_shortcut: float32 [192, 512], replicated
- grad_first_shortcut_gain: float32 [512], replicated
- grad_first_shortcut_shift: float32 [512], replicated
- grad_second_reduce: float32 [512, 512], replicated
- grad_second_reduce_gain: float32 [512], replicated
- grad_second_reduce_shift: float32 [512], replicated
- grad_second_groups: float32 [9, 8, 64, 64], replicated
- grad_second_groups_gain: float32 [512], replicated
- grad_second_groups_shift: float32 [512], replicated
- grad_second_squeeze: float32 [512, 128], replicated
- grad_second_squeeze_bias: float32 [128], replicated
- grad_second_excite: float32 [128, 512], replicated
- grad_second_excite_bias: float32 [512], replicated
- grad_second_expand: float32 [512, 512], replicated
- grad_second_expand_gain: float32 [512], replicated
- grad_second_expand_shift: float32 [512], replicated
Inputs may be any that keep to these rules, and one draw needn't show every extreme that they name: `valid_rows`: in every micro-batch at least one image has all 32 rows valid. `valid_cols`: in every micro-batch at least one image has all 32 columns valid.
All inputs are finite; a program needn't handle non-finite values.
Results may differ from a plain program's by a relative error of at most 0.023.
Values may be sent and summed in bfloat16 or wider, within the bound.
A program may use at most 128 MiB of HBM per device.

v0:
```python
import functools

import jax
import jax.numpy as jnp
from jax import lax
from jax.experimental import pallas as pl
from jax.experimental.pallas import tpu as pltpu
from jax.sharding import PartitionSpec as P

epsilon = 1e-05
f32 = jnp.float32
bf16 = jnp.bfloat16
MESH = pl.DeviceIdType.MESH
PHASES = ((0, 0), (0, 1), (1, 0), (1, 1))
ORDER = (4, 3, 5, 1, 7, 0, 2, 6, 8)
EXCHANGES = 12
NAMES = (
    "g1", "b1", "gg1", "gb1", "exb1", "eg1", "eb1", "sg1", "sb1", "sqb1",
    "g2", "b2", "gg2", "gb2", "exb2", "eg2", "eb2", "sqb2",
)
VEC = {name: k for k, name in enumerate(NAMES)}
VEC_ROWS = 32
VECTORS = "vec"
LAST_TAP = "k9"


def segments_of(cin, width, taps, group, sq1, sq2, devices):
    layout = (
        (("e2", width), ("sq2", sq2), ("ex2", sq2)),
        (("k2", (taps - 1) * group), ("w2", width)),
        (("e1", width), ("s1", cin), ("sq1", sq1), ("ex1", sq1), (LAST_TAP, group)),
        (("k1", taps * group), (VECTORS, VEC_ROWS)),
        (("w1", cin),),
    )
    starts, segments, at = {}, [], 0
    for parts in layout:
        base = at
        for name, rows in parts:
            starts[name] = (at, rows // 16)
            at += rows // 16 * (width // 128)
        units = -(-(at - base) // devices)
        first = units // 2 * devices if len(segments) < len(layout) - 1 else 0
        segments.append((base, units * devices, at, first))
        at = base + units * devices
    return starts, tuple(segments), at


def sigmoid(v):
    return 0.5 * jnp.tanh(0.5 * v) + 0.5


def silu(v):
    return v * sigmoid(v)


def slope(v):
    s = sigmoid(v)
    return s * (1.0 + v * (1.0 - s))


def dot(left, right):
    return jnp.dot(left, right, preferred_element_type=f32)


def dot_nt(left, right):
    return lax.dot_general(left, right, (((1,), (1,)), ((), ())), preferred_element_type=f32)


def dot_tn(left, right):
    return lax.dot_general(left, right, (((0,), (0,)), ((), ())), preferred_element_type=f32)


def parts_of(v):
    high = v.astype(bf16).astype(f32)
    return high, v - high


def stacked(rows, width):
    ids = lax.broadcasted_iota(jnp.int32, (16, width), 0)
    total = jnp.zeros((16, width), f32)
    for k, row in enumerate(rows):
        total = jnp.where(ids == k, jnp.broadcast_to(row, (16, width)), total)
    return total.astype(bf16)


def small_dot(row, weight, form):
    out = form(stacked(parts_of(row), row.shape[1]), weight)
    return out[0:1] + out[1:2]


def small_outer(left, right):
    lh, ll = parts_of(left)
    rh, rl = parts_of(right)
    return dot_tn(
        stacked((lh, ll, lh, ll), left.shape[1]), stacked((rh, rh, rl, rl), right.shape[1])
    )


def fold(v):
    return v[0] + v[1]


def column(acc):
    return jnp.sum(acc, axis=0, keepdims=True)


class Plan:
    def __init__(self, mesh_sizes, args):
        self.S, self.I, self.R = mesh_sizes
        x, og, w1, k1, sq1, sq2 = args
        self.M, _, self.rows, self.cols, self.cin = x
        _, _, self.hrows, self.side, self.width = og
        self.taps, self.groups, self.gw, _ = k1
        self.q1, self.q2 = sq1[0], sq2[1]
        self.each = self.M // self.S
        self.copies = self.R // self.each
        self.pix = self.side * self.side
        self.band = self.pix // self.cols
        self.bands = 2 * self.side // self.band
        self.starts, self.segments, self.blocks = segments_of(
            self.cin, self.width, self.taps, self.gw, self.q1, self.q2, self.S * self.I * self.R
        )
        self.X = 1
        while self.X * self.X < self.R:
            self.X *= 2
        self.Y = self.R // self.X
        self.sizes = {"s": self.S, "x": self.X, "y": self.Y, "r": self.R, "i": self.I}
        self.streams = []
        self.members = []
        self.rooms = [0] * 4
        for base, size, _, first in self.segments:
            halves = [(base, first, "sxyi"), (base + first, size - first, "syxi")]
            if not first:
                halves = [(base, size, "sri")]
            self.members.append(range(len(self.streams), len(self.streams) + len(halves)))
            for start, count, order in halves:
                self.streams.append((start, count, order, tuple(self.rooms)))
                for level, axis in enumerate(order):
                    self.rooms[level] += count
                    count //= self.sizes[axis]

    def piece(self, stream, level):
        _, size, order, _ = self.streams[stream]
        for axis in order[: level + 1]:
            size //= self.sizes[axis]
        return size


def main_kernel(plan, names, *refs):
    ref = dict(zip(names, refs))
    S, I, R = plan.S, plan.I, plan.R
    side, width, pix, cin = plan.side, plan.width, plan.pix, plan.cin
    half_width = width // 2
    s, i, r = lax.axis_index("section"), lax.axis_index("img"), lax.axis_index("row")
    mine = s * plan.each + r // plan.copies
    waits = []

    barrier = pltpu.get_barrier_semaphore()
    peers = []
    for ds in range(S):
        for dr in range(R):
            if ds or dr:
                peers.append((lax.rem(s + ds, S), i, lax.rem(r + dr, R)))
    for di in range(1, I):
        peers.append((s, lax.rem(i + di, I), r))
    for peer in peers:
        pl.semaphore_signal(barrier, inc=1, device_id=peer, device_id_type=MESH)

    own = []
    loads = {}

    def load(*which):
        for name in which:
            at = (NAMES + WEIGHTS).index(name)
            loads[name] = pltpu.make_async_copy(ref[name], ref[name + "_v"], ref["loads"].at[at])
            loads[name].start(priority=int(name[0] == "k"))

    def need(name):
        if name in loads:
            loads.pop(name).wait()
        return ref[name + "_v"]

    load("w1", "g1", "b1", "k1", "k2")
    for name, rows in (("x", plan.rows), ("og", plan.hrows)):
        copy = pltpu.make_async_copy(
            ref[name].at[mine, 0],
            ref[name + "_in"].at[pl.ds(r * rows, rows)],
            ref[name + "_r"].at[r],
        )
        copy.start()
        own.append(copy)
    pl.semaphore_wait(barrier, len(peers))
    for name, rows in (("x", plan.rows), ("og", plan.hrows)):
        for d in range(1, R):
            t = lax.rem(r + d, R)
            copy = pltpu.make_async_remote_copy(
                src_ref=ref[name].at[s * plan.each + t // plan.copies, 0],
                dst_ref=ref[name + "_in"].at[pl.ds(r * rows, rows)],
                send_sem=ref[name + "_s"].at[d - 1],
                recv_sem=ref[name + "_r"].at[r],
                device_id=(s, i, t),
                device_id_type=MESH,
            )
            copy.start()
            waits.append(copy.wait_send)

    load("s1", *NAMES[2:], "sq1", "ex1", "e1", "w2", "sq2", "ex2", "e2")

    def arrived(name, rows, position, d):
        if d == 0:
            own[position].wait()
        else:
            t = lax.rem(r + d, R)
            there = ref[name + "_in"].at[pl.ds(t * rows, rows)]
            pltpu.make_async_remote_copy(
                src_ref=there,
                dst_ref=there,
                send_sem=ref[name + "_s"].at[d - 1],
                recv_sem=ref[name + "_r"].at[t],
                device_id=(s, i, t),
                device_id_type=MESH,
            ).wait_recv()

    st = ref["st"]

    def pairs_of(k):
        return 2 if k in (0, 1, 9) else 1

    def stats_copy(k, d, slot):
        return pltpu.make_async_remote_copy(
            src_ref=st.at[k, slot, pl.ds(0, pairs_of(k))],
            dst_ref=st.at[k, slot, pl.ds(0, pairs_of(k))],
            send_sem=ref["st_s"].at[k, d - 1],
            recv_sem=ref["st_r"].at[k, slot],
            device_id=(s, lax.rem(i + d, I), r),
            device_id_type=MESH,
        )

    def post(k, rows):
        ids = lax.broadcasted_iota(jnp.int32, (8, 128), 0)
        rows = [*rows, *([None] * (len(rows) % 2))]
        for pair in range(len(rows) // 2):
            value = jnp.zeros((8, 128), f32)
            for j in range(8):
                row = rows[2 * pair + j // 4]
                if row is not None:
                    piece = row[:, 128 * (j % 4) : 128 * (j % 4) + 128]
                    value = jnp.where(ids == j, jnp.broadcast_to(piece, (8, 128)), value)
            st[k, i, pair] = value
        for d in range(1, I):
            stats_copy(k, d, i).start()

    def fetch(k, count=2):
        for d in range(1, I):
            stats_copy(k, d, i).wait_send()
            stats_copy(k, d, lax.rem(i + d, I)).wait_recv()
        out = []
        for pair in range((count + 1) // 2):
            value = st[k, 0, pair]
            for j in range(1, I):
                value = value + st[k, j, pair]
            for half in range(2):
                out.append(
                    jnp.concatenate(
                        [
                            jnp.broadcast_to(value[4 * half + j : 4 * half + j + 1], (8, 128))
                            for j in range(4)
                        ],
                        axis=1,
                    )
                )
        return out

    vec = ref["vec"]

    def keep_vectors():
        for name in NAMES:
            row = need(name)[...].astype(f32)
            size = row.shape[0]
            vec[VEC[name], :, :size] = jnp.broadcast_to(row.reshape(1, size), (8, size))

    def vector(name):
        return vec[VEC[name]]

    vr, vc = ref["vr"][0, mine], ref["vc"][0, mine]
    q_ids = lax.broadcasted_iota(jnp.int32, (side, width), 0)
    first_col, last_col = q_ids == 0, q_ids == side - 1
    cm = ref["cm"]
    for b in range(2):
        cm[b] = (2 * q_ids + b < vc).astype(f32)

    def line(value):
        return value.astype(f32).reshape(2, 8, width)

    def pixels(value):
        return value.reshape(side, width)

    def mask_row(a, b, p):
        return line(cm[b]) * (2 * p + a < vr).astype(f32)

    def wide(row):
        return jnp.broadcast_to(row, (8, width))

    row_count = jnp.full((1, width), vr * vc, jnp.int32).astype(f32)
    half_count = jnp.full((1, width), ((vr + 1) // 2) * ((vc + 1) // 2), jnp.int32).astype(f32)

    def over_rows(step, *accs):
        init = tuple(jnp.zeros((8, width), f32) for _ in range(accs[0] if accs else 0))

        def run(p, carry):
            out = step(p)
            if not carry:
                return carry
            return tuple(c + fold(o) for c, o in zip(carry, out))

        return tuple(column(c) for c in lax.fori_loop(0, side, run, init, unroll=16))

    def full_dot(out, left, weight, form=dot):
        wide = out.shape[-1]
        step = min(256, wide)
        for h in range(wide // step):
            cut = slice(h * step, h * step + step)
            w = weight[:, cut] if form is dot else weight[cut, :]
            out[:, :, cut] = form(left, w).reshape(side, side, step).astype(out.dtype)

    hm = ref["hm"]
    for p in range(side):
        hm[p * side : (p + 1) * side] = cm[0][:, :128] * (2 * p < vr).astype(f32)

    def with_moments(out, products):
        sums = []
        for h, product in enumerate(products):
            span = product.shape[1]
            value = product.astype(out.dtype)
            out[:, :, h * span : (h + 1) * span] = value.reshape(side, side, span)
            value = value.astype(f32)
            valid = value * jnp.concatenate([hm[...]] * (span // 128), axis=1)
            sums.append(
                [
                    jnp.sum(x.reshape(pix // 8, 8, span), axis=0)
                    for x in (valid, valid * value)
                ]
            )
        return [column(jnp.concatenate(x, axis=1)) for x in zip(*sums)]

    def dot_moments(out, left, weight):
        return with_moments(
            out, (dot(left, weight[:, cut : cut + 256]) for cut in range(0, width, 256))
        )

    def flat(value):
        return value.reshape(pix, value.shape[-1])

    def lines(ref_, start=0):
        return flat(ref_[start : start + side])

    G, F = ref["local"], ref["grads"]
    lead = None if plan.copies == 1 else (lax.rem(r, plan.copies) == 0).astype(f32)

    def put(name, value, row=0, lane=0):
        if lead is not None:
            value = value * lead
        start, per_tile = plan.starts[name]
        count = value.shape[0] // 16
        for k in range(value.shape[1] // 128):
            piece = value[:, 128 * k : 128 * k + 128].astype(bf16).reshape(count, 16, 128)
            at = start + (lane // 128 + k) * per_tile + row // 16
            G[at : at + count] = piece

    X, Y = plan.X, plan.Y
    x, y = lax.rem(r, X), r // X
    axes = {
        "s": (S, s, lambda t: (t, i, r)),
        "r": (R, r, lambda t: (s, i, t)),
        "x": (X, x, lambda t: (s, i, y * X + t)),
        "y": (Y, y, lambda t: (s, i, t * X + x)),
        "i": (I, i, lambda t: (s, t, r)),
    }

    def scatter_source(stream, level):
        base, _, order, offsets = plan.streams[stream]
        if level == 0:
            return G, base
        return ref[f"sum{level - 1}"], offsets[level]

    def scatter_copies(stream, level, outgoing):
        base, size, order, offsets = plan.streams[stream]
        count, me, device = axes[order[level]]
        piece = plan.piece(stream, level)
        source, first = scatter_source(stream, level)
        for d in range(1, count):
            t = lax.rem(me + d, count)
            slot = me if outgoing else t
            copy = pltpu.make_async_remote_copy(
                src_ref=source.at[pl.ds(first + t * piece, piece)],
                dst_ref=ref[f"got{level}"].at[pl.ds(offsets[level] + slot * piece, piece)],
                send_sem=ref["rs_s"].at[stream, level, d - 1],
                recv_sem=ref["rs_r"].at[stream, level, slot],
                device_id=device(t),
                device_id_type=MESH,
            )
            if outgoing:
                copy.start()
                sent[stream].append(copy)
            else:
                copy.wait_recv()

    def add_up(stream, level):
        base, size, order, offsets = plan.streams[stream]
        count, me, _ = axes[order[level]]
        piece = plan.piece(stream, level)
        source, first = scatter_source(stream, level)
        got = ref[f"got{level}"]
        if level < len(order) - 1:
            out, at = ref[f"sum{level}"], offsets[level + 1]
        else:
            out, at = F, own_part(stream, len(order))
        step = next(k for k in (16, 12, 10, 9, 8, 7, 6, 5, 4, 3, 2, 1) if piece % k == 0)

        def run(k, carry):
            total = source[pl.ds(first + me * piece + k * step, step)].astype(f32)
            for d in range(1, count):
                t = lax.rem(me + d, count)
                total = total + got[pl.ds(offsets[level] + t * piece + k * step, step)].astype(f32)
            out[pl.ds(at + k * step, step)] = total.astype(bf16)
            return carry

        lax.fori_loop(0, piece // step, run, 0)

    def own_part(stream, depth):
        at, _, order, _ = plan.streams[stream]
        for level in range(depth):
            at = at + axes[order[level]][1] * plan.piece(stream, level)
        return at

    def gather_copies(stream, level, outgoing):
        count, me, device = axes[plan.streams[stream][2][level]]
        base = own_part(stream, level)
        piece = plan.piece(stream, level)
        for d in range(1, count):
            t = lax.rem(me + d, count)
            slot = me if outgoing else t
            there = F.at[pl.ds(base + slot * piece, piece)]
            copy = pltpu.make_async_remote_copy(
                src_ref=there,
                dst_ref=there,
                send_sem=ref["ag_s"].at[stream, level, d - 1],
                recv_sem=ref["ag_r"].at[stream, level, slot],
                device_id=device(t),
                device_id_type=MESH,
            )
            if outgoing:
                copy.start()
                sent[stream].append(copy)
            else:
                copy.wait_recv()

    done = [0] * len(plan.segments)
    started = []
    sent = [[] for _ in plan.streams]

    def pump(*which):
        for g in which or tuple(started):
            if g not in started:
                started.insert(0, g)
            k = done[g]
            depth = len(plan.streams[plan.members[g][0]][2])
            if k > 2 * depth:
                continue
            done[g] += 1
            if k == 0:
                base, size, used, _ = plan.segments[g]
                if used < base + size:
                    G[used : base + size] = jnp.zeros((base + size - used, 16, 128), bf16)
            for stream in plan.members[g]:
                if 1 <= k <= depth:
                    scatter_copies(stream, k - 1, False)
                    add_up(stream, k - 1)
                elif k > depth:
                    gather_copies(stream, 2 * depth - k, False)
                for copy in sent[stream]:
                    copy.wait_send()
                sent[stream] = []
                if k < depth:
                    scatter_copies(stream, k, True)
                elif k < 2 * depth:
                    gather_copies(stream, 2 * depth - 1 - k, True)

    vec_grads = {}

    gw = plan.gw
    span = 4 * gw
    def blocks(name, out, turned=False):
        kernels = need(name)
        shape = (span, gw) if turned else (gw, span)
        long = lax.broadcasted_iota(jnp.int32, shape, 0 if turned else 1)
        short = lax.broadcasted_iota(jnp.int32, shape, 1 if turned else 0)
        spread = (lax.rem(long, gw) == short).astype(f32).astype(bf16)
        row = lax.broadcasted_iota(jnp.int32, (span, span), 0) // gw
        col = lax.broadcasted_iota(jnp.int32, (span, span), 1) // gw
        for k, t in enumerate(ORDER):
            for h in range(width // span):
                piece = kernels[t, 4 * h : 4 * h + 4].reshape(span, gw)
                full = dot_nt(spread, piece) if turned else dot(piece, spread)
                out[h, k * span : (k + 1) * span] = jnp.where(row == col, full, 0.0).astype(bf16)

    def groups_grad(name, taps, turned):
        lane = lax.broadcasted_iota(jnp.int32, (gw, span), 1) // gw
        for t, (var, start) in enumerate(taps):
            for h in range(width // span):
                cut = slice(h * span, (h + 1) * span)
                res = dot(turned[h], flat(var[start : start + side, :, cut]))
                out = res[0:gw]
                for j in range(1, 4):
                    out = jnp.where(lane == j, res[j * gw : (j + 1) * gw], out)
                if name == "k2" and t == plan.taps - 1:
                    put(LAST_TAP, out, 0, h * span)
                else:
                    put(name, out, t * gw, h * span)

    band, bands = plan.band, plan.bands
    bhalf = band // 2
    out_id = lax.broadcasted_iota(jnp.int32, (pix, pix), 0)
    in_id = lax.broadcasted_iota(jnp.int32, (pix, pix), 1)

    def source(o):
        quarter = o // (bhalf * side)
        down = lax.rem(o, bhalf * side) // side
        return (2 * down + quarter // 2) * plan.cols + 2 * lax.rem(o, side) + lax.rem(quarter, 2)

    ref["sort"][...] = (source(out_id) == in_id).astype(f32).astype(bf16)
    ref["unsort"][...] = (source(in_id) == out_id).astype(f32).astype(bf16)

    xp, R1 = ref["xp"], ref["R1"]
    keep_vectors()

    def transpose(source, out):
        out[...] = source.astype(f32).T.astype(bf16)

    totals = [jnp.zeros((8, width), f32)] * 2
    by_band = plan.rows % band == 0
    if not by_band:
        for d in range(R):
            arrived("x", plan.rows, 0, d)
    for d in range(bands):
        if by_band:
            if d % (plan.rows // band) == 0:
                arrived("x", plan.rows, 0, d // (plan.rows // band))
            k = lax.rem(r * (plan.rows // band) + d, bands)
        else:
            k = d
        block = ref["x_in"][pl.ds(k * band, band)].reshape(pix, cin)
        block = dot(ref["sort"][...], block).astype(bf16)
        xp[k] = block.reshape(4 * bhalf, side, cin)
        full_dot(R1.at[k], block, need("w1"))
        for j in range(4 * bhalf):
            a, b = PHASES[j // bhalf]
            v = line(R1[k, j])
            mv = v * mask_row(a, b, k * bhalf + j % bhalf)
            totals = [totals[0] + fold(mv), totals[1] + fold(mv * v)]
    even = xp.at[:, 0:bhalf]

    def at_phase(ab, p):
        return p // bhalf, ab * bhalf + lax.rem(p, bhalf)

    post(0, [column(totals[0]), column(totals[1]), row_count, half_count])
    SC = ref["SC"]
    short_sums = dot_moments(SC, even[...].reshape(pix, cin), need("s1"))

    blocks("k1", ref["bd1"])

    def coefficients(first, second, inverse, gain, shift):
        mean = first * inverse
        scale = lax.rsqrt(second * inverse - mean * mean + epsilon)
        a = scale * gain
        return a, shift - mean * a, scale, -mean * scale

    tot = fetch(0, 4)
    inv_full, inv_half = 1.0 / tot[2], 1.0 / tot[3]
    n1 = coefficients(tot[0], tot[1], inv_full, vector("g1"), vector("b1"))

    va = ref["va"]
    va[3:6, 0:1] = jnp.zeros((3, 1, side, width), bf16)

    def shifted(v, edge, amount):
        return jnp.where(edge, 0.0, pltpu.roll(v, amount, 0))

    for ab, (a, b) in enumerate(PHASES):

        def step(p, ab=ab, a=a, b=b):
            v = mask_row(a, b, p) * silu(line(R1[at_phase(ab, p)]) * n1[0] + n1[1])
            v = pixels(v)
            slot = (0, 1, 3, 4)[ab]
            va[slot, p + a] = v.astype(bf16)
            if b:
                va[slot + 1, p + a] = shifted(v, first_col, 1).astype(bf16)

        over_rows(step)
    taps1 = []
    for t in range(9):
        u, v = t // 3, t % 3
        slot = (0, 1, 3, 4)[2 * (u != 1) + (v != 1)] + (v == 0)
        taps1.append((va.at[slot], 1 if u == 2 else 0))

    def convolve(taps, weights, out):
        def half(h):
            cut = slice(h * span, (h + 1) * span)
            left = [flat(taps[t][0][taps[t][1] : taps[t][1] + side, :, cut]) for t in ORDER]
            return dot(jnp.concatenate(left, axis=1), weights[h])

        return with_moments(out, (half(h) for h in range(width // span)))

    c1 = ref["c1"]
    post(1, [*convolve(taps1, ref["bd1"], c1), *short_sums])
    blocks("k2", ref["bd2"])
    tot = fetch(1, 4)
    nc1 = coefficients(tot[0], tot[1], inv_half, vector("gg1"), vector("gb1"))
    ns = coefficients(tot[2], tot[3], inv_half, vector("sg1"), vector("sb1"))

    def excite(conv, norm, hidden, gated, sq, sq_form, sqb, ex, exb):
        def step(p):
            v = mask_row(0, 0, p) * silu(line(conv[p]) * norm[0] + norm[1])
            hidden[p] = pixels(v)
            return (v,)

        (total,) = over_rows(step, 1)
        pooled = total / half_count
        pre = small_dot(pooled, sq[...], sq_form) + sqb
        inner = silu(pre)
        gate = sigmoid(small_dot(inner, ex[...], dot) + exb)
        gate_wide = wide(gate)

        def step_two(p):
            gated[p] = pixels(line(hidden[p]) * gate_wide).astype(bf16)

        over_rows(step_two)
        return pooled, pre, inner, gate

    H1, ga1 = ref["H1"], ref["ga1"]
    kept1 = excite(
        c1, nc1, H1, ga1, need("sq1"), dot_nt, vec[VEC["sqb1"], 0:1, : plan.q1], need("ex1"), vec[VEC["exb1"], 0:1]
    )
    E1 = ref["E1"]
    post(2, dot_moments(E1, lines(ga1), need("e1")))
    transpose(lines(ga1), ref["ga1t"])
    tot = fetch(2)
    ne = coefficients(tot[0], tot[1], inv_half, vector("eg1"), vector("eb1"))
    ent = ref["ent"]
    both_shifts = ne[1] + ns[1]

    def step(p):
        v = line(E1[p]) * ne[0] + line(SC[p]) * ns[0] + both_shifts
        ent[p] = pixels(mask_row(0, 0, p) * silu(v)).astype(bf16)

    over_rows(step)

    def send_out(source, out, rows, target, steps=None):
        for k in range(R // plan.copies) if steps is None else steps:
            t = lax.rem(r + plan.copies * k, R)
            there = ref[out].at[0, mine, 0] if out == "act" else ref[out].at[mine, 0]
            here = source.at[pl.ds(t * rows, rows)]
            copy = pltpu.make_async_remote_copy(
                src_ref=here,
                dst_ref=there,
                send_sem=ref[out + "_s"].at[target, k],
                recv_sem=ref[out + "_r"].at[mine],
                device_id=(target, i, t),
                device_id_type=MESH,
            )
            if k:
                copy.start()
                waits.append(copy.wait_send)
            else:
                local = pltpu.make_async_copy(here, there, ref[out + "_r"].at[mine])

                @pl.when(s == target)
                def _():
                    local.start()

                @pl.when(s != target)
                def _():
                    copy.start()

                def finish(copy=copy):
                    @pl.when(s != target)
                    def _():
                        copy.wait_send()

                waits.append(finish)

    send_out(ent, "act", plan.hrows, 0)

    R2 = ref["R2"]
    post(3, dot_moments(R2, lines(ent), need("w2")))
    transpose(lines(ent), ref["entt"])
    for k in range(bands):
        transpose(xp[k].reshape(pix, cin), ref["xpt"].at[k])
    tot = fetch(3)
    n2 = coefficients(tot[0], tot[1], inv_half, vector("g2"), vector("b2"))
    vb = ref["vb"]
    vb[:, 0:1] = jnp.zeros((3, 1, side, width), bf16)
    vb[:, side + 1 :] = jnp.zeros((3, 1, side, width), bf16)

    def three(out, p, v):
        out[0, p + 1] = shifted(v, first_col, 1).astype(bf16)
        out[1, p + 1] = v.astype(bf16)
        out[2, p + 1] = shifted(v, last_col, side - 1).astype(bf16)

    def step(p):
        three(vb, p, pixels(mask_row(0, 0, p) * silu(line(R2[p]) * n2[0] + n2[1])))

    over_rows(step)
    taps2 = [(vb.at[t % 3], t // 3) for t in range(9)]
    c2 = ref["c2"]
    post(4, convolve(taps2, ref["bd2"], c2))
    blocks("k2", ref["bd2t"], True)
    tot = fetch(4)
    nc2 = coefficients(tot[0], tot[1], inv_half, vector("gg2"), vector("gb2"))
    H2, ga2 = ref["H2"], ref["ga2"]
    kept2 = excite(
        c2, nc2, H2, ga2, need("sq2"), dot, vec[VEC["sqb2"], 0:1, : plan.q2], need("ex2"), vec[VEC["exb2"], 0:1]
    )
    E2 = ref["E2"]
    post(5, dot_moments(E2, lines(ga2), need("e2")))
    transpose(lines(ga2), ref["ga2t"])
    for d in range(R):
        arrived("og", plan.hrows, 1, d)
    tot = fetch(5)
    ne2 = coefficients(tot[0], tot[1], inv_half, vector("eg2"), vector("eb2"))
    leave, D, og = ref["leave"], ref["D"], ref["og_in"]

    def step(p):
        e = line(E2[p])
        v = e * ne2[0] + ne2[1] + line(ent[p])
        sg = sigmoid(v)
        m = mask_row(0, 0, p)
        leave[p] = pixels(m * v * sg).astype(bf16)
        g = line(og[p]) * m * (sg * (1.0 + v * (1.0 - sg)))
        D[p] = pixels(g)
        return g, g * (e * ne2[2] + ne2[3])

    parts = over_rows(step, 2)
    vec_grads["eb2"], vec_grads["eg2"] = parts
    post(6, parts)
    send_out(leave, "act", plan.hrows, 1)
    blocks("k1", ref["bd1t"], True)

    def back_rule(sums, inverse, gain, norm):
        a = gain * norm[2]
        k0 = a * (sums[0] + norm[3] * sums[1]) * inverse
        return a, k0, a * norm[2] * sums[1] * inverse

    def back_excite(dg, kept, hidden, conv, norm, sq, sq_form, ex, out):
        pooled, pre, inner, gate = kept

        def step(p):
            return (line(dg[p]) * line(hidden[p]),)

        (dgate,) = over_rows(step, 1)
        dpre = dgate * gate * (1.0 - gate)
        dsq = small_dot(dpre, ex[...], dot_nt) * slope(pre)
        dpool = wide(small_dot(dsq, sq[...], sq_form) / half_count)
        gate_wide = wide(gate)

        def step_two(p):
            v = line(conv[p])
            g = (line(dg[p]) * gate_wide + dpool) * mask_row(0, 0, p)
            g = g * slope(v * norm[0] + norm[1])
            out[p] = pixels(g)
            return g, g * (v * norm[2] + norm[3])

        return over_rows(step_two, 2), dpre, dsq

    def excite_grads(name, kept, dpre, dsq):
        pooled, pre, inner, gate = kept
        put("sq" + name, small_outer(dsq, pooled))
        put("ex" + name, small_outer(inner, dpre))
        vec_grads["exb" + name] = dpre
        count = dsq.shape[1]
        eye = (
            lax.broadcasted_iota(jnp.int32, (count, width), 0)
            == lax.broadcasted_iota(jnp.int32, (count, width), 1)
        ).astype(f32).astype(bf16)
        vec_grads["sqb" + name] = small_dot(dsq, eye, dot)

    def turn(gradient_ref, start):
        out = []
        for h in range(width // span):
            piece = flat(gradient_ref[start : start + side, :, h * span : (h + 1) * span])
            out.append(piece.astype(f32).T.astype(bf16))
        return out

    d1, dg, GR = ref["d1"], ref["dg"], ref["GR"]
    tot = fetch(6)
    rule = back_rule((tot[0], tot[1]), inv_half, vector("eg2"), ne2)

    def step(p):
        v = rule[0] * line(D[p]) - mask_row(0, 0, p) * (rule[1] + rule[2] * line(E2[p]))
        d1[p] = pixels(v).astype(bf16)

    over_rows(step)
    full_dot(dg, lines(d1), need("e2"), dot_nt)
    parts, dpre, dsq = back_excite(dg, kept2, H2, c2, nc2, need("sq2"), dot_nt, need("ex2"), GR)
    vec_grads["gb2"], vec_grads["gg2"] = parts
    post(7, parts)
    put("e2", dot(ref["ga2t"][...], lines(d1)))
    excite_grads("2", kept2, dpre, dsq)
    pump(0)
    tot = fetch(7)
    rule = back_rule((tot[0], tot[1]), inv_half, vector("gg2"), nc2)
    vd = ref["vd"]
    vd[:, 0:1] = jnp.zeros((3, 1, side, width), bf16)
    vd[:, side + 1 :] = jnp.zeros((3, 1, side, width), bf16)

    def step(p):
        v = rule[0] * line(GR[p]) - mask_row(0, 0, p) * (rule[1] + rule[2] * line(c2[p]))
        three(vd, p, pixels(v))

    over_rows(step)

    def convolve_back(taps, first, weights, out):
        for h in range(width // span):
            cut = slice(h * span, (h + 1) * span)
            left = [flat(var[start : start + side, :, cut]) for var, start in taps]
            rows = slice(first * span, (first + len(taps)) * span)
            acc = dot(jnp.concatenate(left, axis=1), weights[h, rows])
            out[:, :, cut] = acc.reshape(side, side, span)

    DA = ref["DA"]
    convolve_back(
        [(vd.at[2 - t % 3], 2 - t // 3) for t in ORDER],
        0,
        ref["bd2t"],
        DA.at[0],
    )

    def step(p):
        v = line(R2[p])
        g = line(DA[0, p]) * mask_row(0, 0, p) * slope(v * n2[0] + n2[1])
        GR[p] = pixels(g)
        return g, g * (v * n2[2] + n2[3])

    parts = over_rows(step, 2)
    vec_grads["b2"], vec_grads["g2"] = parts
    post(8, parts)
    pump(0)
    groups_grad("k2", taps2, turn(vd.at[1], 1))
    tot = fetch(8)
    rule = back_rule((tot[0], tot[1]), inv_half, vector("g2"), n2)

    def step(p):
        v = rule[0] * line(GR[p]) - mask_row(0, 0, p) * (rule[1] + rule[2] * line(R2[p]))
        d1[p] = pixels(v).astype(bf16)

    over_rows(step)
    full_dot(GR, lines(d1), need("w2"), dot_nt)
    pump(0)

    def step(p):
        e, sc = line(E1[p]), line(SC[p])
        g = line((D[p] + GR[p]).astype(bf16))
        g = g * mask_row(0, 0, p) * slope(e * ne[0] + sc * ns[0] + both_shifts)
        D[p] = pixels(g)
        return g, g * (e * ne[2] + ne[3]), g * (sc * ns[2] + ns[3])

    parts = over_rows(step, 3)
    vec_grads["eb1"], vec_grads["eg1"], vec_grads["sg1"] = parts
    vec_grads["sb1"] = parts[0]
    post(9, parts)
    put("w2", dot(ref["entt"][...], lines(d1)))
    pump(1, 0)
    tot = fetch(9, 3)
    rule_e = back_rule((tot[0], tot[1]), inv_half, vector("eg1"), ne)
    rule_s = back_rule((tot[0], tot[2]), inv_half, vector("sg1"), ns)
    d2 = ref["d2"]

    def step(p):
        g, m = line(D[p]), mask_row(0, 0, p)
        v = rule_e[0] * g - m * (rule_e[1] + rule_e[2] * line(E1[p]))
        d1[p] = pixels(v).astype(bf16)
        v = rule_s[0] * g - m * (rule_s[1] + rule_s[2] * line(SC[p]))
        d2[p] = pixels(v).astype(bf16)

    over_rows(step)
    full_dot(dg, lines(d1), need("e1"), dot_nt)
    pump(1)
    parts, dpre, dsq = back_excite(dg, kept1, H1, c1, nc1, need("sq1"), dot, need("ex1"), GR)
    vec_grads["gb1"], vec_grads["gg1"] = parts
    post(10, parts)
    put("e1", dot(ref["ga1t"][...], lines(d1)))
    put("s1", dot_tn(even[...].reshape(pix, cin), lines(d2)))
    excite_grads("1", kept1, dpre, dsq)
    pump(2, 1)
    tot = fetch(10)
    rule = back_rule((tot[0], tot[1]), inv_half, vector("gg1"), nc1)

    def step(p):
        v = rule[0] * line(GR[p]) - mask_row(0, 0, p) * (rule[1] + rule[2] * line(c1[p]))
        three(vd, p, pixels(v))

    over_rows(step)
    pump(0)
    sums = []
    for ab, (a, b) in enumerate(PHASES):
        chosen = []
        first = (0, 1, 3, 5)[ab]
        for t in ORDER[first : first + (1, 2, 2, 4)[ab]]:
            chosen.append((vd.at[2 if t % 3 == 0 else 1], 2 if t // 3 == 0 else 1))
        convolve_back(chosen, first, ref["bd1t"], DA.at[ab])

        def step(p, ab=ab, a=a, b=b):
            v = line(R1[at_phase(ab, p)])
            g = line(DA[ab, p]) * mask_row(a, b, p) * slope(v * n1[0] + n1[1])
            DA[ab, p] = pixels(g)
            return g, g * (v * n1[2] + n1[3])

        sums.append(over_rows(step, 2))
        if ab == 1:
            pump(2, 1)
        elif ab == 3:
            pump(0)
    parts = (sum(x[0] for x in sums), sum(x[1] for x in sums))
    vec_grads["b1"], vec_grads["g1"] = parts
    post(11, parts)
    pump(2)
    groups_grad("k1", taps1, turn(vd.at[1], 1))
    ids = lax.broadcasted_iota(jnp.int32, (VEC_ROWS, width), 0)
    value = jnp.zeros((VEC_ROWS, width), f32)
    for name, at in VEC.items():
        value = jnp.where(ids == at, jnp.broadcast_to(vec_grads[name], value.shape), value)
    put(VECTORS, value)
    pump(3, 2, 0)
    tot = fetch(11)
    rule = back_rule((tot[0], tot[1]), inv_full, vector("g1"), n1)
    dr = ref["dr"]
    for ab, (a, b) in enumerate(PHASES):

        def step(p, ab=ab, a=a, b=b):
            v = rule[0] * line(DA[ab, p])
            v = v - mask_row(a, b, p) * (rule[1] + rule[2] * line(R1[at_phase(ab, p)]))
            dr[at_phase(ab, p)] = pixels(v).astype(bf16)

        over_rows(step)
    total = None
    for k in range(bands):
        term = dot(ref["xpt"][k], dr[k].reshape(pix, width))
        total = term if total is None else total + term
    put("w1", total)
    pump(4, 3, 1)
    cut = cin // 2
    ref["dxo0"][...] = jnp.zeros((2 * side, plan.cols, 128), bf16)
    ref["dxo1"][...] = jnp.zeros((2 * side, plan.cols, 128), bf16)
    stepwise = plan.each == bands
    for d in [*range(1, bands), 0]:
        k = lax.rem(r + plan.copies * d, R) * plan.rows // band if stepwise else d
        for part in range(2):
            dxo = ref[f"dxo{part}"]
            rows = slice(part * cut, (part + 1) * cut)
            v = dot_nt(dr[k].reshape(pix, width), need("w1")[rows, :])
            w = dot_nt(
                d2[pl.ds(k * bhalf, bhalf)].reshape(bhalf * side, width), need("s1")[rows, :]
            )
            v = jnp.concatenate([v[: bhalf * side] + w, v[bhalf * side :]], axis=0)
            v = dot(ref["unsort"][...], v.astype(bf16)).astype(bf16)
            dxo[pl.ds(k * band, band), :, :cut] = v.reshape(band, plan.cols, cut)
            if stepwise:
                send_out(dxo, "dx", plan.rows, part, (d,))
        pump(*((4, 3, 2, 1), (4, 3, 1), (4, 3, 2), (1, 0))[(d - 1) % 4])
    if not stepwise:
        send_out(ref["dxo0"], "dx", plan.rows, 0)
        send_out(ref["dxo1"], "dx", plan.rows, 1)
    for _ in range(9):
        pump()
    for wait in waits:
        wait()
    for m in range(plan.M):
        t = (m % plan.each) * plan.copies + lax.rem(r, plan.copies)
        for out in ("act", "dx"):
            there = ref[out].at[0, m, 0] if out == "act" else ref[out].at[m, 0]
            pltpu.make_async_copy(there, there, ref[out + "_r"].at[m]).wait()


WEIGHTS = ("w1", "k1", "k2", "sq1", "ex1", "e1", "s1", "w2", "sq2", "ex2", "e2")


def run_main(plan, arrays):
    side, width, cin = plan.side, plan.width, plan.cin
    wide = 4 * plan.gw
    field = (side, side, width)
    scratch = {
        "x_in": pltpu.VMEM((2 * side, plan.cols, cin), bf16),
        "og_in": pltpu.VMEM(field, bf16),
        "st": pltpu.VMEM((EXCHANGES, plan.I, 2, 8, 128), f32),
        "hm": pltpu.VMEM((plan.pix, 128), f32),
        "cm": pltpu.VMEM((2, side, width), f32),
        **{
            name: pltpu.VMEM((width // wide, plan.taps * wide, wide), bf16)
            for name in ("bd1", "bd2", "bd1t", "bd2t")
        },
        "xpt": pltpu.VMEM((plan.bands, cin, plan.pix), bf16),
        **{name: pltpu.VMEM((width, plan.pix), bf16) for name in ("ga1t", "ga2t", "entt")},
        "sort": pltpu.VMEM((plan.pix, plan.pix), bf16),
        "unsort": pltpu.VMEM((plan.pix, plan.pix), bf16),
        "xp": pltpu.VMEM((plan.bands, 2 * plan.band, side, cin), bf16),
        "R1": pltpu.VMEM((plan.bands, 2 * plan.band, side, width), f32),
        "va": pltpu.VMEM((6, side + 1, side, width), bf16),
        "vb": pltpu.VMEM((3, side + 2, side, width), bf16),
        "vd": pltpu.VMEM((3, side + 2, side, width), bf16),
        "DA": pltpu.VMEM((4,) + field, f32),
        "dr": pltpu.VMEM((plan.bands, 2 * plan.band, side, width), bf16),
        "dxo0": pltpu.VMEM((2 * side, plan.cols, 128), bf16),
        "dxo1": pltpu.VMEM((2 * side, plan.cols, 128), bf16),
    }
    for name in ("SC", "H1", "E1", "R2", "H2", "E2", "D", "GR"):
        scratch[name] = pltpu.VMEM(field, f32)
    for name in ("c1", "ga1", "ent", "c2", "ga2", "leave", "d1", "d2", "dg"):
        scratch[name] = pltpu.VMEM(field, bf16)
    for name in ("x", "og"):
        scratch[name + "_s"] = pltpu.SemaphoreType.DMA((max(plan.R - 1, 1),))
        scratch[name + "_r"] = pltpu.SemaphoreType.DMA((plan.R,))
    scratch["st_s"] = pltpu.SemaphoreType.DMA((EXCHANGES, max(plan.I - 1, 1)))
    scratch["st_r"] = pltpu.SemaphoreType.DMA((EXCHANGES, plan.I))
    for name in ("act", "dx"):
        scratch[name + "_s"] = pltpu.SemaphoreType.DMA((2, plan.R // plan.copies))
        scratch[name + "_r"] = pltpu.SemaphoreType.DMA((plan.M,))
    for name in NAMES + WEIGHTS:
        scratch[name + "_v"] = pltpu.VMEM(arrays[name].shape, bf16)
    scratch["vec"] = pltpu.VMEM((len(NAMES), 8, width), f32)
    scratch["loads"] = pltpu.SemaphoreType.DMA((len(NAMES + WEIGHTS),))
    scratch["local"] = pltpu.VMEM((plan.blocks, 16, 128), bf16)
    for level, room in enumerate(plan.rooms):
        scratch[f"got{level}"] = pltpu.VMEM((room, 16, 128), bf16)
        if level:
            scratch[f"sum{level - 1}"] = pltpu.VMEM((room, 16, 128), bf16)
    most = max(plan.sizes.values())
    for name in ("rs", "ag"):
        scratch[name + "_s"] = pltpu.SemaphoreType.DMA((len(plan.streams), 4, most - 1))
        scratch[name + "_r"] = pltpu.SemaphoreType.DMA((len(plan.streams), 4, most))
    inputs = ("x", "og", "vr", "vc") + NAMES + WEIGHTS
    outputs = ("act", "dx", "grads")
    names = inputs + outputs + tuple(scratch)
    any_space = pl.BlockSpec(memory_space=pl.ANY)
    smem = pl.BlockSpec(memory_space=pltpu.SMEM)
    vmem = pl.BlockSpec(memory_space=pltpu.VMEM)
    return pl.pallas_call(
        functools.partial(main_kernel, plan, names),
        out_shape=(
            jax.ShapeDtypeStruct((1, plan.M, 1, plan.hrows, side, width), bf16),
            jax.ShapeDtypeStruct((plan.M, 1, plan.rows, plan.cols, 128), bf16),
            pltpu.VMEM((plan.blocks, 16, 128), bf16),
        ),
        in_specs=[any_space, any_space, smem, smem] + [any_space] * (len(NAMES) + len(WEIGHTS)),
        out_specs=(any_space, any_space, vmem),
        scratch_shapes=list(scratch.values()),
        compiler_params=pltpu.CompilerParams(
            collective_id=0, has_side_effects=True, vmem_limit_bytes=58 * 1024 * 1024
        ),
        name="blocks",
    )(*[arrays[name] for name in inputs])


OUTS = (
    "w1", "g1", "b1", "k1", "gg1", "gb1", "sq1", "sqb1", "ex1", "exb1", "e1", "eg1", "eb1",
    "s1", "sg1", "sb1", "w2", "g2", "b2", "k2", "gg2", "gb2", "sq2", "sqb2", "ex2", "exb2",
    "e2", "eg2", "eb2",
)


def unpack_kernel(plan, blocks, act_in, dx_in, *rest):
    count = len(OUTS) + 2
    outs, bufs, through, sems = rest[:count], rest[count:-2], rest[-2], rest[-1]
    copies = []
    for k, whole in enumerate((act_in, dx_in)):
        copies.append(pltpu.make_async_copy(whole, bufs[k - 2], through.at[k]))
        copies[-1].start()
    order = sorted(plan.starts, key=lambda name: plan.starts[name])
    order = [name for name in order if name not in (VECTORS, LAST_TAP)]

    def tile(name, k):
        start, per_tile = plan.starts[name]
        at = start + k * per_tile
        return blocks[at : at + per_tile].reshape(16 * per_tile, 128).astype(f32)

    tiles = plan.width // 128
    vec = None
    turn = [OUTS.index(name) for name in order]
    turn += [k for k, name in enumerate(OUTS) if name in VEC]
    for position, k in enumerate(turn):
        name, out = OUTS[k], bufs[k]
        if position < 2:
            copies[position].wait()
            copies[position] = pltpu.make_async_copy(
                bufs[position - 2], outs[position], sems.at[position]
            )
            copies[position].start()
        if name in VEC and vec is None:
            vec = jnp.concatenate([tile(VECTORS, k) for k in range(tiles)], axis=1)
        if name in VEC:
            size = out.shape[0]
            out[...] = vec[VEC[name] : VEC[name] + 1, :size].reshape(size)
        elif name[0] == "k":

            def run(t, carry, name=name, out=out, last_tap=False):
                for lane in range(tiles):
                    start, per_tile = plan.starts[name]
                    at = start + lane * per_tile + t * (plan.gw // 16)
                    if last_tap:
                        start, per_tile = plan.starts[LAST_TAP]
                        at = start + lane * per_tile
                    piece = blocks[pl.ds(at, plan.gw // 16)].reshape(plan.gw, 128)
                    piece = piece.astype(f32).T
                    for j in range(128 // plan.gw):
                        group = lane * (128 // plan.gw) + j
                        out[t, group, :, : plan.gw] = piece[j * plan.gw : (j + 1) * plan.gw]
                return carry

            if name == "k2":
                lax.fori_loop(0, plan.taps - 1, run, 0)
                run(plan.taps - 1, 0, last_tap=True)
            else:
                lax.fori_loop(0, plan.taps, run, 0)
        elif name == "sq2":
            for lane in range(tiles):
                out[128 * lane : 128 * lane + 128] = tile(name, lane).T
        else:
            for lane in range(tiles):
                out[:, 128 * lane : 128 * lane + 128] = tile(name, lane)
        copies.append(pltpu.make_async_copy(out, outs[k + 2], sems.at[k + 2]))
        copies[-1].start()
    for copy in copies:
        copy.wait()


def unpack(plan, act, dx, grads, weights):
    shapes = []
    for name, w in zip(OUTS, weights):
        shape = w.shape[:3] + (128,) if name[0] == "k" else w.shape
        shapes.append(jax.ShapeDtypeStruct(shape, f32))
    any_space = pl.BlockSpec(memory_space=pl.ANY)
    return pl.pallas_call(
        functools.partial(unpack_kernel, plan),
        out_shape=[jax.ShapeDtypeStruct(v.shape, v.dtype) for v in (act, dx)] + shapes,
        in_specs=[pl.BlockSpec(memory_space=pltpu.VMEM)]
        + [pl.BlockSpec(memory_space=pltpu.HBM)] * 2,
        out_specs=[any_space] * (len(shapes) + 2),
        scratch_shapes=[pltpu.VMEM(v.shape, v.dtype) for v in (*shapes, act, dx)]
        + [pltpu.SemaphoreType.DMA((2,))]
        + [pltpu.SemaphoreType.DMA((len(shapes) + 2,))],
        compiler_params=pltpu.CompilerParams(vmem_limit_bytes=24 * 1024 * 1024),
        name="unpack",
    )(grads, act, dx)


def body(sizes, input_maps, valid_rows, valid_cols, *rest):
    weights, output_grad = rest[:-1], rest[-1]
    (w1, g1, b1, k1, gg1, gb1, sq1, sqb1, ex1, exb1, e1, eg1, eb1, s1, sg1, sb1) = weights[:16]
    (w2, g2, b2, k2, gg2, gb2, sq2, sqb2, ex2, exb2, e2, eg2, eb2) = weights[16:]
    turned = sq1.T
    plan = Plan(sizes, [v.shape for v in (input_maps, output_grad, w1, k1, turned, sq2)])
    vectors = (
        g1, b1, gg1, gb1, exb1, eg1, eb1, sg1, sb1, sqb1, g2, b2, gg2, gb2, exb2, eg2, eb2, sqb2,
    )
    arrays = dict(
        x=input_maps, og=output_grad, vr=valid_rows.T, vc=valid_cols.T, w1=w1,
        k1=k1, k2=k2,
        sq1=turned, ex1=ex1, e1=e1, s1=s1, w2=w2, sq2=sq2, ex2=ex2, e2=e2,
        **dict(zip(NAMES, vectors)),
    )
    act, dx, grads = run_main(plan, arrays)
    act, dx, *out = unpack(plan, act, dx, grads, weights[:6] + (turned,) + weights[7:])
    out[6] = out[6].T
    for at in (3, 19):
        out[at] = out[at][..., : plan.gw]
    dx = dx[..., : plan.cin // 2]
    return (act, dx, *out)


def solution(mesh):
    tiled = P(None, "img", "row", None, None)
    image = P(None, "img")
    sizes = tuple(mesh.shape[name] for name in ("section", "img", "row"))
    return jax.shard_map(
        functools.partial(body, sizes),
        mesh=mesh,
        in_specs=(tiled, image, image) + (P(),) * 29 + (tiled,),
        out_specs=(
            P("section", None, "img", "row", None, None),
            P(None, "img", "row", None, "section"),
        )
        + (P(),) * 29,
        check_vma=False,
    )
```

profile of v0, /device:TPU:0, one launch (start us, length us, event | category | flops | bytes accessed | tf_op | source)
XLA Modules:
  0.0 115.2 jit_solution(5577305857117964827)
XLA Ops:
  0.7 107.6 %blocks.1 = (bf16[1,8,1,4,16,512]{5,4,3,2,1,0:T(8,128)(2,1)}, bf16[8,1,8,32,128]{4,3,2,1,0:T(8,128)(2,1)}, bf16[896,16,128]{2,1,0:T(8,128)(2,1)S(1)}) custom-call(bf16[8,1,8,32,192]{4,3,2,1,0:T(8,128)(2,1)} %refs_0_.1, bf16[8,1,4,16,512]{4,3,2,1,0:T(8,128)(2,1)} %refs_1_.1, s32[1,8]{1,0:T(1,128)} %bitcast.8, s32[1,8]{1,0:T(1,128)} %bitcast.9, ...), custom_call_target="tpu_custom_call" | custom-call | tf_op jit(solution)/shard_map/blocks/pallas_call | solution.py:1045
  108.3 0.0 copy-start
  108.3 1.0 copy-done
  109.3 0.0 copy-start.1
  109.3 1.0 copy-done.1
  110.4 4.7 %unpack.1 = (bf16[1,8,1,4,16,512]{5,4,3,2,1,0:T(8,128)(2,1)}, bf16[8,1,8,32,128]{4,3,2,1,0:T(8,128)(2,1)}, f32[192,512]{1,0:T(8,128)}, f32[512]{0:T(512)}, f32[5...) custom-call(bf16[896,16,128]{2,1,0:T(8,128)(2,1)S(1)} %get-tuple-ele, ...), custom_call_target="tpu_custom_call" | custom-call | tf_op jit(solution)/shard_map/unpack/pallas_call | solution.py:1140
Async XLA Ops:
  108.3 1.0 copy-start
  109.3 1.0 copy-start.1
where the time goes:
time: 115 us
  Pallas kernels  112 us (97%)
  local copies, waits for them, and re-layouts  2.08 us (2%)
    pallas_call x1, Pallas kernels, run_main(): pl.pallas_call(functools.partial(main_kernel, plan, names), out_shape=(ja...  108 us
    pallas_call x1, Pallas kernels, unpack(): pl.pallas_call(functools.partial(unpack_kernel, plan), out_shape=[jax.Sha...  4.72 us

commit v1 on v0

--- a/solution.py
+++ b/solution.py
@@ -249,10 +249,14 @@
             st[k, i, pair] = value
         for d in range(1, I):
             stats_copy(k, d, i).start()
+        for d in range(1, I):
+            if k:
+                stats_copy(k - 1, d, i).wait_send()
+            if k == EXCHANGES - 1:
+                waits.append(stats_copy(k, d, i).wait_send)
 
     def fetch(k, count=2):
         for d in range(1, I):
-            stats_copy(k, d, i).wait_send()
             stats_copy(k, d, lax.rem(i + d, I)).wait_recv()
         out = []
         for pair in range((count + 1) // 2):
@@ -1045,12 +1049,12 @@
     return pl.pallas_call(
         functools.partial(main_kernel, plan, names),
         out_shape=(
-            jax.ShapeDtypeStruct((1, plan.M, 1, plan.hrows, side, width), bf16),
-            jax.ShapeDtypeStruct((plan.M, 1, plan.rows, plan.cols, 128), bf16),
+            pltpu.VMEM((1, plan.M, 1, plan.hrows, side, width), bf16),
+            pltpu.VMEM((plan.M, 1, plan.rows, plan.cols, 128), bf16),
             pltpu.VMEM((plan.blocks, 16, 128), bf16),
         ),
         in_specs=[any_space, any_space, smem, smem] + [any_space] * (len(NAMES) + len(WEIGHTS)),
-        out_specs=(any_space, any_space, vmem),
+        out_specs=(vmem, vmem, vmem),
         scratch_shapes=list(scratch.values()),
         compiler_params=pltpu.CompilerParams(
             collective_id=0, has_side_effects=True, vmem_limit_bytes=58 * 1024 * 1024
@@ -1068,10 +1072,10 @@
 
 def unpack_kernel(plan, blocks, act_in, dx_in, *rest):
     count = len(OUTS) + 2
-    outs, bufs, through, sems = rest[:count], rest[count:-2], rest[-2], rest[-1]
+    outs, bufs, sems = rest[:count], rest[count:-1], rest[-1]
     copies = []
     for k, whole in enumerate((act_in, dx_in)):
-        copies.append(pltpu.make_async_copy(whole, bufs[k - 2], through.at[k]))
+        copies.append(pltpu.make_async_copy(whole, outs[k], sems.at[k]))
         copies[-1].start()
     order = sorted(plan.starts, key=lambda name: plan.starts[name])
     order = [name for name in order if name not in (VECTORS, LAST_TAP)]
@@ -1085,14 +1089,8 @@
     vec = None
     turn = [OUTS.index(name) for name in order]
     turn += [k for k, name in enumerate(OUTS) if name in VEC]
-    for position, k in enumerate(turn):
+    for k in turn:
         name, out = OUTS[k], bufs[k]
-        if position < 2:
-            copies[position].wait()
-            copies[position] = pltpu.make_async_copy(
-                bufs[position - 2], outs[position], sems.at[position]
-            )
-            copies[position].start()
         if name in VEC and vec is None:
             vec = jnp.concatenate([tile(VECTORS, k) for k in range(tiles)], axis=1)
         if name in VEC:
@@ -1140,11 +1138,9 @@
     return pl.pallas_call(
         functools.partial(unpack_kernel, plan),
         out_shape=[jax.ShapeDtypeStruct(v.shape, v.dtype) for v in (act, dx)] + shapes,
-        in_specs=[pl.BlockSpec(memory_space=pltpu.VMEM)]
-        + [pl.BlockSpec(memory_space=pltpu.HBM)] * 2,
+        in_specs=[pl.BlockSpec(memory_space=pltpu.VMEM)] * 3,
         out_specs=[any_space] * (len(shapes) + 2),
-        scratch_shapes=[pltpu.VMEM(v.shape, v.dtype) for v in (*shapes, act, dx)]
-        + [pltpu.SemaphoreType.DMA((2,))]
+        scratch_shapes=[pltpu.VMEM(v.shape, v.dtype) for v in shapes]
         + [pltpu.SemaphoreType.DMA((len(shapes) + 2,))],
         compiler_params=pltpu.CompilerParams(vmem_limit_bytes=24 * 1024 * 1024),
         name="unpack",

time: 115 us -> 113 us (0.983)
  local copies, waits for them, and re-layouts: 2.08 us -> 0 us
    unnamed x4 -> x0, local copies, waits for them, and re-layouts: 2.08 us -> none
where the time goes in v1:
time: 113 us
  Pallas kernels  112 us (99%)
    pallas_call x1, Pallas kernels, run_main(): pl.pallas_call(functools.partial(main_kernel, plan, names), out_shape=(pl...  108 us
    pallas_call x1, Pallas kernels, unpack(): pl.pallas_call(functools.partial(unpack_kernel, plan), out_shape=[jax.Sha...  4.61 us

profile of v1, /device:TPU:0, one launch (start us, length us, event | category | flops | bytes accessed | tf_op | source)
XLA Modules:
  0.0 113.1 jit_solution(2077637667882044144)
XLA Ops:
  0.7 107.6 %blocks.1 = (bf16[1,8,1,4,16,512]{5,4,3,2,1,0:T(8,128)(2,1)S(1)}, bf16[8,1,8,32,128]{4,3,2,1,0:T(8,128)(2,1)S(1)}, bf16[896,16,128]{2,1,0:T(8,128)(2,1)S(1)}) custom-call(bf16[8,1,8,32,192]{4,3,2,1,0:T(8,128)(2,1)} %refs_0_.1, bf16[8,1,4,16,512]{4,3,2,1,0:T(8,128)(2,1)} %refs_1_.1, s32[1,8]{1,0:T(1,128)} %bitcast.8, s32[1,8]{1,0:T(1,128)} %bitcast.9, ...), custom_call_target="tpu_custom_call" | custom-call | tf_op jit(solution)/shard_map/blocks/pallas_call | solution.py:1049
  108.3 4.6 %unpack.1 = (bf16[1,8,1,4,16,512]{5,4,3,2,1,0:T(8,128)(2,1)}, bf16[8,1,8,32,128]{4,3,2,1,0:T(8,128)(2,1)}, f32[192,512]{1,0:T(8,128)}, f32[512]{0:T(512)}, f32[5...) custom-call(bf16[896,16,128]{2,1,0:T(8,128)(2,1)S(1)} %get-tuple-ele, ...), custom_call_target="tpu_custom_call" | custom-call | tf_op jit(solution)/shard_map/unpack/pallas_call | solution.py:1138

commit v2 on v1

--- a/solution.py
+++ b/solution.py
@@ -180,7 +180,7 @@
             loads.pop(name).wait()
         return ref[name + "_v"]
 
-    load("w1", "g1", "b1", "k1", "k2")
+    load("w1", "g1", "b1", "k1")
     for name, rows in (("x", plan.rows), ("og", plan.hrows)):
         copy = pltpu.make_async_copy(
             ref[name].at[mine, 0],
@@ -204,7 +204,7 @@
             copy.start()
             waits.append(copy.wait_send)
 
-    load("s1", *NAMES[2:], "sq1", "ex1", "e1", "w2", "sq2", "ex2", "e2")
+    load("s1", "k2", *NAMES[2:], "sq1", "ex1", "e1", "w2", "sq2", "ex2", "e2")
 
     def arrived(name, rows, position, d):
         if d == 0:
@@ -616,7 +616,8 @@
 
     c1 = ref["c1"]
     post(1, [*convolve(taps1, ref["bd1"], c1), *short_sums])
-    blocks("k2", ref["bd2"])
+    for k in range(bands):
+        transpose(xp[k].reshape(pix, cin), ref["xpt"].at[k])
     tot = fetch(1, 4)
     nc1 = coefficients(tot[0], tot[1], inv_half, vector("gg1"), vector("gb1"))
     ns = coefficients(tot[2], tot[3], inv_half, vector("sg1"), vector("sb1"))
@@ -647,6 +648,7 @@
     E1 = ref["E1"]
     post(2, dot_moments(E1, lines(ga1), need("e1")))
     transpose(lines(ga1), ref["ga1t"])
+    blocks("k2", ref["bd2"])
     tot = fetch(2)
     ne = coefficients(tot[0], tot[1], inv_half, vector("eg1"), vector("eb1"))
     ent = ref["ent"]
@@ -697,16 +699,15 @@
     R2 = ref["R2"]
     post(3, dot_moments(R2, lines(ent), need("w2")))
     transpose(lines(ent), ref["entt"])
-    for k in range(bands):
-        transpose(xp[k].reshape(pix, cin), ref["xpt"].at[k])
     tot = fetch(3)
     n2 = coefficients(tot[0], tot[1], inv_half, vector("g2"), vector("b2"))
     vb = ref["vb"]
     vb[:, 0:1] = jnp.zeros((3, 1, side, width), bf16)
     vb[:, side + 1 :] = jnp.zeros((3, 1, side, width), bf16)
 
-    def three(out, p, v):
-        out[0, p + 1] = shifted(v, first_col, 1).astype(bf16)
+    def three(out, p, v, both=True):
+        if both:
+            out[0, p + 1] = shifted(v, first_col, 1).astype(bf16)
         out[1, p + 1] = v.astype(bf16)
         out[2, p + 1] = shifted(v, last_col, side - 1).astype(bf16)
 
@@ -900,7 +901,7 @@
 
     def step(p):
         v = rule[0] * line(GR[p]) - mask_row(0, 0, p) * (rule[1] + rule[2] * line(c1[p]))
-        three(vd, p, pixels(v))
+        three(vd, p, pixels(v), both=False)
 
     over_rows(step)
     pump(0)
@@ -1079,6 +1080,7 @@
         copies[-1].start()
     order = sorted(plan.starts, key=lambda name: plan.starts[name])
     order = [name for name in order if name not in (VECTORS, LAST_TAP)]
+    order.sort(key=lambda name: -16 * plan.starts[name][1])
 
     def tile(name, k):
         start, per_tile = plan.starts[name]

time: 113 us -> 114 us (level)
  no operation moved by 1% of the time
where the time goes in v2:
time: 114 us; the launch traced here: 113 us
  Pallas kernels  113 us (99%)
    pallas_call x1, Pallas kernels, run_main(): pl.pallas_call(functools.partial(main_kernel, plan, names), out_shape=(pl...  108 us
    pallas_call x1, Pallas kernels, unpack(): pl.pallas_call(functools.partial(unpack_kernel, plan), out_shape=[jax.Sha...  4.91 us

profile of v2, /device:TPU:0, one launch (start us, length us, event | category | flops | bytes accessed | tf_op | source)
XLA Modules:
  0.0 113.4 jit_solution(1571682737255640031)
XLA Ops:
  0.7 107.7 %blocks.1 = (bf16[1,8,1,4,16,512]{5,4,3,2,1,0:T(8,128)(2,1)S(1)}, bf16[8,1,8,32,128]{4,3,2,1,0:T(8,128)(2,1)S(1)}, bf16[896,16,128]{2,1,0:T(8,128)(2,1)S(1)}) custom-call(bf16[8,1,8,32,192]{4,3,2,1,0:T(8,128)(2,1)} %refs_0_.1, bf16[8,1,4,16,512]{4,3,2,1,0:T(8,128)(2,1)} %refs_1_.1, s32[1,8]{1,0:T(1,128)} %bitcast.8, s32[1,8]{1,0:T(1,128)} %bitcast.9, ...), custom_call_target="tpu_custom_call" | custom-call | tf_op jit(solution)/shard_map/blocks/pallas_call | solution.py:1050
  108.3 4.9 %unpack.1 = (bf16[1,8,1,4,16,512]{5,4,3,2,1,0:T(8,128)(2,1)}, bf16[8,1,8,32,128]{4,3,2,1,0:T(8,128)(2,1)}, f32[192,512]{1,0:T(8,128)}, f32[512]{0:T(512)}, f32[5...) custom-call(bf16[896,16,128]{2,1,0:T(8,128)(2,1)S(1)} %get-tuple-ele, ...), custom_call_target="tpu_custom_call" | custom-call | tf_op jit(solution)/shard_map/unpack/pallas_call | solution.py:1140

commit v3 on v1

--- a/solution.py
+++ b/solution.py
@@ -39,7 +39,7 @@
             starts[name] = (at, rows // 16)
             at += rows // 16 * (width // 128)
         units = -(-(at - base) // devices)
-        first = units // 2 * devices if len(segments) < len(layout) - 1 else 0
+        first = units // 2 * devices if 0 < len(segments) < len(layout) - 1 else 0
         segments.append((base, units * devices, at, first))
         at = base + units * devices
     return starts, tuple(segments), at
@@ -837,6 +837,7 @@
         ref["bd2t"],
         DA.at[0],
     )
+    pump(0)
 
     def step(p):
         v = line(R2[p])
@@ -847,7 +848,6 @@
     parts = over_rows(step, 2)
     vec_grads["b2"], vec_grads["g2"] = parts
     post(8, parts)
-    pump(0)
     groups_grad("k2", taps2, turn(vd.at[1], 1))
     tot = fetch(8)
     rule = back_rule((tot[0], tot[1]), inv_half, vector("g2"), n2)
@@ -858,7 +858,6 @@
 
     over_rows(step)
     full_dot(GR, lines(d1), need("w2"), dot_nt)
-    pump(0)
 
     def step(p):
         e, sc = line(E1[p]), line(SC[p])
@@ -887,14 +886,13 @@
 
     over_rows(step)
     full_dot(dg, lines(d1), need("e1"), dot_nt)
-    pump(1)
     parts, dpre, dsq = back_excite(dg, kept1, H1, c1, nc1, need("sq1"), dot, need("ex1"), GR)
     vec_grads["gb1"], vec_grads["gg1"] = parts
     post(10, parts)
     put("e1", dot(ref["ga1t"][...], lines(d1)))
     put("s1", dot_tn(even[...].reshape(pix, cin), lines(d2)))
     excite_grads("1", kept1, dpre, dsq)
-    pump(2, 1)
+    pump(2, 1, 0)
     tot = fetch(10)
     rule = back_rule((tot[0], tot[1]), inv_half, vector("gg1"), nc1)
 
@@ -903,7 +901,6 @@
         three(vd, p, pixels(v))
 
     over_rows(step)
-    pump(0)
     sums = []
     for ab, (a, b) in enumerate(PHASES):
         chosen = []
@@ -920,20 +917,18 @@
 
         sums.append(over_rows(step, 2))
         if ab == 1:
-            pump(2, 1)
-        elif ab == 3:
-            pump(0)
+            pump(2)
     parts = (sum(x[0] for x in sums), sum(x[1] for x in sums))
     vec_grads["b1"], vec_grads["g1"] = parts
     post(11, parts)
-    pump(2)
+    pump(1, 0)
     groups_grad("k1", taps1, turn(vd.at[1], 1))
     ids = lax.broadcasted_iota(jnp.int32, (VEC_ROWS, width), 0)
     value = jnp.zeros((VEC_ROWS, width), f32)
     for name, at in VEC.items():
         value = jnp.where(ids == at, jnp.broadcast_to(vec_grads[name], value.shape), value)
     put(VECTORS, value)
-    pump(3, 2, 0)
+    pump(3, 1)
     tot = fetch(11)
     rule = back_rule((tot[0], tot[1]), inv_full, vector("g1"), n1)
     dr = ref["dr"]
@@ -950,7 +945,7 @@
         term = dot(ref["xpt"][k], dr[k].reshape(pix, width))
         total = term if total is None else total + term
     put("w1", total)
-    pump(4, 3, 1)
+    pump(4, 2)
     cut = cin // 2
     ref["dxo0"][...] = jnp.zeros((2 * side, plan.cols, 128), bf16)
     ref["dxo1"][...] = jnp.zeros((2 * side, plan.cols, 128), bf16)
@@ -969,7 +964,7 @@
             dxo[pl.ds(k * band, band), :, :cut] = v.reshape(band, plan.cols, cut)
             if stepwise:
                 send_out(dxo, "dx", plan.rows, part, (d,))
-        pump(*((4, 3, 2, 1), (4, 3, 1), (4, 3, 2), (1, 0))[(d - 1) % 4])
+        pump(*((3, 1), (4, 3, 2, 1), (4, 3, 2, 1, 0), (4, 3, 2))[(d - 1) % 4])
     if not stepwise:
         send_out(ref["dxo0"], "dx", plan.rows, 0)
         send_out(ref["dxo1"], "dx", plan.rows, 1)

time: 113 us -> 113 us (level)
  no operation moved by 1% of the time
where the time goes in v3:
time: 113 us
  Pallas kernels  112 us (99%)
    pallas_call x1, Pallas kernels, run_main(): pl.pallas_call(functools.partial(main_kernel, plan, names), out_shape=(pl...  107 us
    pallas_call x1, Pallas kernels, unpack(): pl.pallas_call(functools.partial(unpack_kernel, plan), out_shape=[jax.Sha...  4.61 us

profile of v3, /device:TPU:0, one launch (start us, length us, event | category | flops | bytes accessed | tf_op | source)
XLA Modules:
  0.0 112.9 jit_solution(10895986923792523096)
XLA Ops:
  0.7 107.4 %blocks.1 = (bf16[1,8,1,4,16,512]{5,4,3,2,1,0:T(8,128)(2,1)S(1)}, bf16[8,1,8,32,128]{4,3,2,1,0:T(8,128)(2,1)S(1)}, bf16[896,16,128]{2,1,0:T(8,128)(2,1)S(1)}) custom-call(bf16[8,1,8,32,192]{4,3,2,1,0:T(8,128)(2,1)} %refs_0_.1, bf16[8,1,4,16,512]{4,3,2,1,0:T(8,128)(2,1)} %refs_1_.1, s32[1,8]{1,0:T(1,128)} %bitcast.8, s32[1,8]{1,0:T(1,128)} %bitcast.9, ...), custom_call_target="tpu_custom_call" | custom-call | tf_op jit(solution)/shard_map/blocks/pallas_call | solution.py:1044
  108.1 4.6 %unpack.1 = (bf16[1,8,1,4,16,512]{5,4,3,2,1,0:T(8,128)(2,1)}, bf16[8,1,8,32,128]{4,3,2,1,0:T(8,128)(2,1)}, f32[192,512]{1,0:T(8,128)}, f32[512]{0:T(512)}, f32[5...) custom-call(bf16[896,16,128]{2,1,0:T(8,128)(2,1)S(1)} %get-tuple-ele, ...), custom_call_target="tpu_custom_call" | custom-call | tf_op jit(solution)/shard_map/unpack/pallas_call | solution.py:1133
